TPU v7x, 32 devices: a whole 2x2x4 slice. The times are simulated.
32 devices in a mesh: groups: 2 (over x), context: 16 (over z, y, core).
Axes of the slice: x: 2, y: 2, z: 4, core: 2. Of those that a mesh axis runs over, the one named last changes fastest.
Arguments:
- q_store: bfloat16 [4096, 4096], P(('groups', 'context')), parts along dimension 0, may hold values from -6 to 6
- k_store: bfloat16 [4096, 4096], P(('groups', 'context')), parts along dimension 0, may hold values from -6 to 6
- v_store: bfloat16 [4096, 4096], P(('groups', 'context')), parts along dimension 0, may hold values from -6 to 6
- plan: int32 [32, 128], P(('groups', 'context')), parts along dimension 0, may hold values from 0 to 127, each once within a row
- doc_ids: int32 [4096], P(('groups', 'context')), parts along dimension 0, may hold values from 0 to 3, never falling along the last dimension, each value on 1 to 1024 neighbouring positions
- gain: float32 [4096], replicated, may hold values from 0.5 to 1.5
Outputs:
- out_store: bfloat16 [4096, 4096], P(('groups', 'context')), parts along dimension 0
There are 2 independent parts, one for each index of `groups`. A program takes and returns all parts, laid end to end along the dimension named above; an argument that names none is the same for every part. Nothing has to cross between parts.
Inputs may be any that keep to these rules, and one draw needn't show every extreme that they name: Each row of plan names every offset below 128 once. `doc_ids`: never falls along positions; each document holds 1 to 1024 positions.
All inputs are finite; a program needn't handle non-finite values.
Results may differ from a plain program's by a relative error of at most 0.005.
Values may be sent and summed in bfloat16 or wider, within the bound.
A program may use at most 320 MiB of HBM per device.

v0:
```python
import jax
import jax.numpy as jnp
from jax import lax
from jax.sharding import PartitionSpec as P

HEAD_DIM = 128
SPAN = 128


def entering(part, axis, combine, identity):
    place = lax.axis_index(axis)
    gathered = jax.tree.map(lambda a: lax.all_gather(a, axis), part)
    state = jax.tree.map(lambda a, e: jnp.zeros_like(a) + jnp.asarray(e, a.dtype), part, identity)

    def one(lap, state):
        return combine(
            state, jax.tree.map(lambda a: lax.dynamic_index_in_dim(a, lap, 0, False), gathered)
        )

    return lax.fori_loop(0, place, one, state)


def merge_states(earlier, later):
    early_state, early_doc = earlier
    late_state, late_doc = later
    keep_early = jnp.logical_or(early_doc == late_doc, late_doc < 0)
    merged = late_state + jnp.where(
        keep_early[:, None, None], early_state, jnp.zeros_like(early_state)
    )
    return (merged, jnp.where(late_doc < 0, early_doc, late_doc))


def on_device(q_store, k_store, v_store, plan, doc_ids, gain):
    token_count = q_store.shape[0]
    head_count = q_store.shape[1] // HEAD_DIM
    span_count = token_count // SPAN
    placed = plan.reshape(-1)
    inverse = (
        jnp.zeros((token_count,), jnp.int32)
        .at[placed]
        .set(jnp.arange(token_count, dtype=jnp.int32))
    )

    def settle(arrived):
        return jnp.take(arrived, inverse, axis=0).reshape(span_count, SPAN, head_count, HEAD_DIM)

    docs = doc_ids.reshape(span_count, SPAN)
    last_doc = docs[:, -1]
    query_rows, key_rows, value_rows = (
        lax.all_to_all(q_store, "context", split_axis=0, concat_axis=0, tiled=True),
        lax.all_to_all(k_store, "context", split_axis=0, concat_axis=0, tiled=True),
        lax.all_to_all(v_store, "context", split_axis=0, concat_axis=0, tiled=True),
    )
    keys_home = settle(key_rows)
    values_home = settle(value_rows)
    tail_mask = (docs == last_doc[:, None]).astype(jnp.bfloat16)
    span_states = jnp.einsum(
        "cshd,cshe->chde",
        keys_home * tail_mask[:, :, None, None],
        values_home,
        preferred_element_type=jnp.float32,
    )
    device_part = (span_states[0], last_doc)
    identity = (jnp.zeros_like(span_states[0]), jnp.full((1,), -1, jnp.int32))
    running = entering(device_part, "context", merge_states, identity)
    carry_list = [running[0].astype(jnp.bfloat16)]
    doc_list = running[1]
    carry_states = jnp.stack(carry_list)
    queries = settle(query_rows)
    causal = jnp.arange(SPAN)[:, None] >= jnp.arange(SPAN)[None, :]
    allowed = jnp.logical_and(causal[None], docs[:, :, None] == docs[:, None, :])
    scores = jnp.einsum("cthd,cshd->chts", queries, keys_home, preferred_element_type=jnp.float32)
    weights = jnp.where(allowed[:, None], scores, 0.0).astype(jnp.bfloat16)
    inner = jnp.einsum("chts,cshe->cthe", weights, values_home, preferred_element_type=jnp.float32)
    match = (docs == doc_list[:, None]).astype(jnp.bfloat16)
    matched = queries * match[:, :, None, None]
    carried = jnp.einsum(
        "cthd,chde->cthe", matched, carry_states, preferred_element_type=jnp.float32
    )
    mixed = inner + carried
    scale = lax.rsqrt(jnp.mean(mixed * mixed, axis=-1, keepdims=True) + 1e-06)
    normed = (mixed * scale * gain.reshape(head_count, HEAD_DIM)).astype(jnp.bfloat16)
    normed = normed.reshape(token_count, head_count * HEAD_DIM)
    leaving = jnp.take(normed, placed, axis=0)
    return lax.all_to_all(leaving, "context", split_axis=0, concat_axis=0, tiled=True)


def solution(mesh):
    return jax.shard_map(
        on_device,
        mesh=mesh,
        in_specs=(
            P(("groups", "context"), None),
            P(("groups", "context"), None),
            P(("groups", "context"), None),
            P(("groups", "context"), None),
            P(("groups", "context")),
            P(),
        ),
        out_specs=P(("groups", "context"), None),
        check_vma=False,
    )
```

profile of v0, /device:TPU:0, one launch (start us, length us, event | category | flops | bytes accessed | tf_op | source)
XLA Modules:
  0.0 390.3 jit_solution(17005539557372690132)
XLA Ops:
  6.5 32.4 %all_to_all.48 = bf16[16,8,4096]{2,1,0:T(8,128)(2,1)S(1)} all-to-all(bf16[16,8,4096]{2,1,0:T(8,128)(2,1)} %bitcast.75), channel_id=1, replica_groups=mesh['groups'=2,'context'=16] {'context'}, dimensions={0} | all-to-all | bytes 2097152 | tf_op jit(solution)/shard_map/all_to_all | solution.py:52
  38.9 29.8 %all_to_all.49 = bf16[16,8,4096]{2,1,0:T(8,128)(2,1)S(1)} all-to-all(bf16[16,8,4096]{2,1,0:T(8,128)(2,1)S(1)} %bitcast.76), channel_id=1, replica_groups=mesh['groups'=2,'context'=16] {'context'}, dimensions={0} | all-to-all | bytes 2097152 | tf_op jit(solution)/shard_map/all_to_all | solution.py:50
  68.7 5.0 %all-to-all-start.2 = ((bf16[16,8,4096]{2,1,0:T(8,128)(2,1)}), bf16[16,8,4096]{2,1,0:T(8,128)(2,1)S(1)}, u32[]{:S(2)}, u32[]{:S(2)}) async-start(bf16[16,8,4096]{2,1,0:T(8,128)(2,1)} %bitcast.77), calls=%async_computation.2 | async-start | bytes 2097152 | tf_op jit(solution)/shard_map/all_to_all | solution.py:51
  73.7 0.0 all-gather.3.cloned.1.call-start
  73.7 0.5 slice.3
  74.3 0.0 copy-done.3
  74.3 1.0 scatter_custom_fusion
  75.3 0.5 compare_convert_fusion.1
  75.9 2.2 gather_fusion
  78.0 2.2 gather_fusion.1
  80.2 16.4 %all-to-all-done.2 = bf16[16,8,4096]{2,1,0:T(8,128)(2,1)S(1)} async-done(((bf16[16,8,4096]{2,1,0:T(8,128)(2,1)}), bf16[16,8,4096]{2,1,0:T(8,128)(2,1)S(1)}, u32[]{:S(2)}, u32[]{:S(2)}) %all-to-all-start.2) | async-done | bytes 1048608 | tf_op jit(solution)/shard_map/all_to_all | solution.py:51
  96.6 2.2 gather_fusion.2
  98.8 3.2 select_bitcast_fusion.2
  102.0 1.6 copy.20
  103.6 1.8 fusion.7
  105.4 0.0 all-gather.3.cloned.1.call-update
  105.5 0.6 copy-done.4
  106.1 0.6 dynamic-slice
  106.7 1.2 bitcast_dynamic-update-slice_fusion
  107.9 13.3 %all-reduce = s32[16]{0:T(128)S(1)} all-reduce(s32[16]{0:T(128)S(1)} %bitcast_dynamic-update-slice_fusion), channel_id=1, replica_groups=mesh['groups'=2,'context'=16] {'context'}, use_global_device_ids=true, to_apply=%add | all-reduce | flops 16 | bytes 128
  121.2 0.1 fusion.20
  121.3 2.5 fusion.3
  123.8 152.2 %all-gather.3.cloned.1.call-done = f32[512,128,128]{2,1,0:T(8,128)} async-done(((f32[32,128,128]{2,1,0:T(8,128)}), f32[512,128,128]{2,1,0:T(8,128)}) %all-gather.3.cloned.1.call-update) | async-done | bytes 33554448 | tf_op jit(solution)/shard_map/all_gather | solution.py:12
  276.0 0.2 broadcast_in_dim.42
  276.3 0.0 copy-start.1
  276.3 2.5 fusion
  278.8 0.7 fusion.2
  279.6 0.5 copy.18
  280.1 1.2 gather_fusion.3
  281.3 0.2 select_bitcast_fusion
  281.5 101.0 %all_to_all.50 = bf16[16,8,4096]{2,1,0:T(8,128)(2,1)S(1)} all-to-all(bf16[16,8,4096]{2,1,0:T(8,128)(2,1)S(1)} %select_bitcast_fusion), channel_id=1, replica_groups=mesh['groups'=2,'context'=16] {'context'}, dimensions={0} | all-to-all | bytes 2097152 | tf_op jit(solution)/shard_map/all_to_all | solution.py:85
  382.5 1.0 copy.55
  (19 shorter events, 0.1 us)
Async XLA Ops:
  6.5 32.4 %copy-start = (bf16[128,4096]{1,0:T(8,128)(2,1)S(1)}, bf16[128,4096]{1,0:T(8,128)(2,1)}, u32[]{:S(2)}) copy-start(bf16[128,4096]{1,0:T(8,128)(2,1)} %param.10) | copy-start | bytes 3145732
  38.9 34.8 %copy-start.2 = (s32[128]{0:T(128)S(1)}, s32[128]{0:T(128)}, u32[]{:S(2)}) copy-start(s32[128]{0:T(128)} %param.14) | copy-start | bytes 1540
  38.9 35.4 %copy-start.3 = (s32[1,128]{1,0:T(1,128)S(1)}, s32[1,128]{1,0:T(1,128)}, u32[]{:S(2)}) copy-start(s32[1,128]{1,0:T(1,128)} %param.13) | copy-start | bytes 1540
  68.7 27.9 %all-to-all-start.2 = ((bf16[16,8,4096]{2,1,0:T(8,128)(2,1)}), bf16[16,8,4096]{2,1,0:T(8,128)(2,1)S(1)}, u32[]{:S(2)}, u32[]{:S(2)}) async-start(bf16[16,8,4096]{2,1,0:T(8,128)(2,1)} %bitcast.77), calls=%async_computation.2 | async-start | bytes 2097152 | tf_op jit(solution)/shard_map/all_to_all | solution.py:51
  73.7 202.3 %all-gather.3.cloned.1.call-start = ((), (), s32[]{:S(2)}) async-start(), calls=%async_computation.4 | async-start | bytes 35651584 | tf_op jit(solution)/shard_map/all_gather | solution.py:12
  105.4 0.7 copy-start.4
  276.3 2.6 copy-start.1
Sparse Core Ops, SparseCore 0:
  105.6 170.3 all-gather.2
where the time goes:
time: 392 us; the launch traced here: 390 us
  blocking collectives  176 us (45%)
  waiting for transfers between devices  169 us (43%)
  local copies, waits for them, and re-layouts  15 us (4%)
  between operations  13.6 us (3%)
  matrix products  6.82 us (2%)
  starting transfers between devices  5.03 us (1%)
  other arithmetic  4.72 us (1%)
    all_gather x1, waiting for transfers between devices, entering(): gathered = jax.tree.map(lambda a: lax.all_gather(a, axis), part)  152 us
    all_to_all x1, blocking collectives, on_device(): lax.all_to_all(leaving, 'context', split_axis=0, concat_axis=0, tiled=True)  101 us
    all_to_all x1, blocking collectives, on_device(): lax.all_to_all(v_store, 'context', split_axis=0, concat_axis=0, tiled=True)  32.4 us
    all_to_all x1, blocking collectives, on_device(): lax.all_to_all(q_store, 'context', split_axis=0, concat_axis=0, tiled=True)  29.8 us
    all_to_all x1, waiting for transfers between devices, on_device(): lax.all_to_all(k_store, 'context', split_axis=0, concat_axis=0, tiled=True)  16.4 us
    unnamed x1, blocking collectives  13.3 us
  transfers between devices with their start and end apart: 2, of which 2 were waited for; matrix products, arithmetic and copies ran while one was open for 3% of the time, Pallas kernels for 0%

commit v1 on v0

--- a/solution.py
+++ b/solution.py
@@ -1,10 +1,203 @@
+import functools
+
 import jax
 import jax.numpy as jnp
 from jax import lax
+from jax.experimental import pallas as pl
+from jax.experimental.pallas import tpu as pltpu
 from jax.sharding import PartitionSpec as P
 
 HEAD_DIM = 128
 SPAN = 128
+TILE = 16
+MESH = pl.DeviceIdType.MESH
+
+
+def flip(me, mask, n):
+    out, bit = 0, 1
+    while bit < n:
+        mine, other = (me // bit) % 2, (mask // bit) % 2
+        out = out + bit * (mine + other - 2 * mine * other)
+        bit *= 2
+    return out
+
+
+def heads_kernel(
+    n, heads, q_ref, k_ref, v_ref, plan_ref, docs_ref, gain_ref, out_ref,
+    got, leaving, info, mask, tail, match, keep, send_sem, got_sem, info_sem, out_sem,
+):
+    tokens = q_ref.shape[0]
+    share = tokens // n
+    blocks = TILE // share
+    rows = n * TILE
+    chunks = tokens // TILE
+    me = lax.axis_index("context")
+    f32, bf16 = jnp.float32, jnp.bfloat16
+
+    barrier = pltpu.get_barrier_semaphore()
+
+    @pl.loop(1, n)
+    def _(step):
+        pl.semaphore_signal(
+            barrier, inc=1, device_id={"context": flip(me, step, n)}, device_id_type=MESH
+        )
+
+    plan = plan_ref[...]
+    here = lax.broadcasted_iota(jnp.int32, (tokens, tokens), 0) == plan
+    docs = jnp.dot(
+        jnp.broadcast_to(docs_ref[...], (8, tokens)).astype(f32).astype(bf16),
+        here.astype(f32).astype(bf16),
+        preferred_element_type=f32,
+    )
+    line = lax.broadcasted_iota(jnp.int32, (8, tokens), 0)
+    lines = jnp.where(line == 0, jnp.broadcast_to(plan, (8, tokens)).astype(f32), docs)
+    turn = me % blocks
+    row = lax.broadcasted_iota(jnp.int32, (tokens, rows), 1)
+    arrived = lax.broadcasted_iota(jnp.int32, (tokens, rows), 0)
+    mine = (row % TILE) // share == turn
+    spread = jnp.logical_and(mine, (row // TILE) * share + row % share == arrived)
+    spread_lines = jnp.dot(
+        lines.astype(bf16), spread.astype(f32).astype(bf16), preferred_element_type=f32
+    )
+    base = jnp.where(
+        jnp.logical_and(mine[:8], lax.broadcasted_iota(jnp.int32, (8, rows), 0) == 0),
+        (turn * tokens).astype(f32),
+        0.0,
+    )
+    info[me] = spread_lines + base
+
+    pl.semaphore_wait(barrier, n - 1)
+
+    @pl.loop(1, n)
+    def _(step):
+        to = flip(me, step, n)
+        pltpu.make_async_remote_copy(
+            src_ref=info.at[me], dst_ref=info.at[me],
+            send_sem=info_sem.at[0], recv_sem=info_sem.at[1],
+            device_id={"context": to}, device_id_type=MESH,
+        ).start()
+
+    def columns(device, g):
+        return pl.ds(pl.multiple_of((device * heads + g) * HEAD_DIM, HEAD_DIM), HEAD_DIM)
+
+    for g in range(heads):
+
+        @pl.loop(1, n)
+        def _(step, g=g):
+            to = flip(me, (step * 7) % n, n)
+            for a, ref in enumerate((q_ref, k_ref, v_ref)):
+                pltpu.make_async_remote_copy(
+                    src_ref=ref.at[:, columns(to, g)], dst_ref=got.at[g, a, me],
+                    send_sem=send_sem.at[g], recv_sem=got_sem.at[g],
+                    device_id={"context": to}, device_id_type=MESH,
+                ).start()
+
+        for a, ref in enumerate((q_ref, k_ref, v_ref)):
+            pltpu.make_async_copy(
+                ref.at[:, columns(me, g)], got.at[g, a, me], got_sem.at[g]
+            ).start()
+
+    def wait_for(ref, sem):
+        pltpu.make_async_copy(ref, ref, sem).wait()
+
+    wait_for(info.at[pl.ds(0, n - 1)], info_sem.at[1])
+    last = jnp.full((1, 1), -1.0, f32)
+    for c in range(chunks):
+        lines = info[c * blocks]
+        for b in range(1, blocks):
+            lines = lines + info[c * blocks + b]
+        upright = lines.T
+        at_row, doc_row = lines[0:1], lines[1:2]
+        at_col, doc_col = upright[:, 0:1], upright[:, 1:2]
+        allowed = jnp.logical_and(at_row <= at_col, doc_row == doc_col)
+        mask[c] = jnp.where(allowed, 1.0, 0.0).astype(bf16)
+        doc_wide = jnp.broadcast_to(doc_col, (rows, HEAD_DIM))
+        match[c] = jnp.where(doc_wide == last, 1.0, 0.0).astype(bf16)
+        latest = jnp.max(doc_row, axis=1, keepdims=True)
+        tail[c] = jnp.where(doc_wide == latest, 1.0, 0.0).astype(bf16)
+        keep[c] = jnp.broadcast_to(jnp.where(last == latest, 1.0, 0.0), (8, HEAD_DIM))
+        last = latest
+
+    for g in range(heads):
+        wait_for(got.at[g], got_sem.at[g])
+        gain = gain_ref[pl.ds(me * heads + g, 1), :]
+        state = jnp.zeros((HEAD_DIM, HEAD_DIM), f32)
+        for c in range(chunks):
+            part = pl.ds(c * TILE, TILE)
+            q = got[g, 0, :, part, :].reshape(rows, HEAD_DIM)
+            k = got[g, 1, :, part, :].reshape(rows, HEAD_DIM)
+            v = got[g, 2, :, part, :].reshape(rows, HEAD_DIM)
+            scores = lax.dot_general(q, k, (((1,), (1,)), ((), ())), preferred_element_type=f32)
+            weights = scores.astype(bf16) * mask[c]
+            mixed = jnp.dot(weights, v, preferred_element_type=f32)
+            if c:
+                mixed = mixed + jnp.dot(
+                    q * match[c], state.astype(bf16), preferred_element_type=f32
+                )
+            if c < chunks - 1:
+                state = state * keep[c, 0:1] + lax.dot_general(
+                    k * tail[c], v, (((0,), (0,)), ((), ())), preferred_element_type=f32
+                )
+            scale = lax.rsqrt(jnp.mean(mixed * mixed, axis=-1, keepdims=True) + 1e-06)
+            leaving[g, :, part, :] = (
+                (mixed * scale * gain).astype(bf16).reshape(n, TILE, HEAD_DIM)
+            )
+
+        @pl.loop(1, n)
+        def _(step, g=g):
+            to = flip(me, (step * 7) % n, n)
+            pltpu.make_async_remote_copy(
+                src_ref=leaving.at[g, to], dst_ref=out_ref.at[:, columns(me, g)],
+                send_sem=send_sem.at[heads + g], recv_sem=out_sem.at[g],
+                device_id={"context": to}, device_id_type=MESH,
+            ).start()
+
+        pltpu.make_async_copy(
+            leaving.at[g, me], out_ref.at[:, columns(me, g)], out_sem.at[g]
+        ).start()
+
+    wait_for(info.at[pl.ds(0, n - 1)], info_sem.at[0])
+    for g in range(heads):
+        wait_for(got.at[g, :, pl.ds(0, n - 1)], send_sem.at[g])
+        wait_for(leaving.at[g, pl.ds(0, n - 1)], send_sem.at[heads + g])
+        wait_for(leaving.at[g], out_sem.at[g])
+
+
+def by_heads(n, q_store, k_store, v_store, plan, doc_ids, gain):
+    tokens, width = q_store.shape
+    heads = width // HEAD_DIM // n
+    rows, chunks = n * TILE, tokens // TILE
+    bf16, f32 = jnp.bfloat16, jnp.float32
+    return pl.pallas_call(
+        functools.partial(heads_kernel, n, heads),
+        out_shape=jax.ShapeDtypeStruct((tokens, width), bf16),
+        in_specs=[pl.BlockSpec(memory_space=pltpu.VMEM)] * 6,
+        out_specs=pl.BlockSpec(memory_space=pltpu.VMEM),
+        scratch_shapes=[
+            pltpu.VMEM((heads, 3, n, tokens, HEAD_DIM), bf16),
+            pltpu.VMEM((heads, n, tokens, HEAD_DIM), bf16),
+            pltpu.VMEM((n, 8, rows), f32),
+            pltpu.VMEM((chunks, rows, rows), bf16),
+            pltpu.VMEM((chunks, rows, HEAD_DIM), bf16),
+            pltpu.VMEM((chunks, rows, HEAD_DIM), bf16),
+            pltpu.VMEM((chunks, 8, HEAD_DIM), f32),
+            pltpu.SemaphoreType.DMA((2 * heads,)),
+            pltpu.SemaphoreType.DMA((heads,)),
+            pltpu.SemaphoreType.DMA((2,)),
+            pltpu.SemaphoreType.DMA((heads,)),
+        ],
+        compiler_params=pltpu.CompilerParams(
+            collective_id=0, has_side_effects=True, vmem_limit_bytes=40 * 1024 * 1024
+        ),
+        cost_estimate=pl.CostEstimate(
+            flops=2 * heads * n * tokens * HEAD_DIM * (2 * rows + 2 * HEAD_DIM),
+            bytes_accessed=8 * tokens * width,
+            transcendentals=heads * n * tokens,
+        ),
+    )(
+        q_store, k_store, v_store, plan.reshape(1, tokens), doc_ids.reshape(1, tokens),
+        gain.reshape(width // HEAD_DIM, HEAD_DIM),
+    )
 
 
 def entering(part, axis, combine, identity):
@@ -30,7 +223,7 @@
     return (merged, jnp.where(late_doc < 0, early_doc, late_doc))
 
 
-def on_device(q_store, k_store, v_store, plan, doc_ids, gain):
+def by_positions(q_store, k_store, v_store, plan, doc_ids, gain):
     token_count = q_store.shape[0]
     head_count = q_store.shape[1] // HEAD_DIM
     span_count = token_count // SPAN
@@ -86,17 +279,22 @@
 
 
 def solution(mesh):
+    n = mesh.shape["context"]
+
+    def on_device(q_store, k_store, v_store, plan, doc_ids, gain):
+        tokens, width = q_store.shape
+        head_count = width // HEAD_DIM
+        share = tokens // n
+        whole = head_count % n == 0 and n & (n - 1) == 0 and n > 1
+        if whole and tokens % TILE == 0 and 0 < share <= TILE and TILE % share == 0:
+            return by_heads(n, q_store, k_store, v_store, plan, doc_ids, gain)
+        return by_positions(q_store, k_store, v_store, plan, doc_ids, gain)
+
+    rows = P(("groups", "context"), None)
     return jax.shard_map(
         on_device,
         mesh=mesh,
-        in_specs=(
-            P(("groups", "context"), None),
-            P(("groups", "context"), None),
-            P(("groups", "context"), None),
-            P(("groups", "context"), None),
-            P(("groups", "context")),
-            P(),
-        ),
-        out_specs=P(("groups", "context"), None),
+        in_specs=(rows, rows, rows, rows, P(("groups", "context")), P()),
+        out_specs=rows,
         check_vma=False,
     )

time: 392 us -> 106 us (0.27)
  blocking collectives: 176 us -> 0 us
  waiting for transfers between devices: 169 us -> 0 us
  Pallas kernels: 0 us -> 100 us
  between operations: 13.6 us -> 0.02 us
  local copies, waits for them, and re-layouts: 15 us -> 6.03 us
  matrix products: 6.82 us -> 0 us
  starting transfers between devices: 5.03 us -> 0 us
  other arithmetic: 4.72 us -> 0 us
    all_to_all x3 -> x0, blocking collectives: 163 us -> none  [the longest x1 101 us: on_device(): lax.all_to_all(leaving, 'context', split_axis=0, concat_axis=0, tiled=True)]
    all_gather x1 -> x0, waiting for transfers between devices: 152 us -> none  [entering(): gathered = jax.tree.map(lambda a: lax.all_gather(a, axis), part)]
    pallas_call x0 -> x1, Pallas kernels: none -> 100 us  [by_heads(): pl.pallas_call(functools.partial(heads_kernel, n, heads), out_shape=jax.S...]
    all_to_all x1 -> x0, waiting for transfers between devices: 16.4 us -> none  [on_device(): lax.all_to_all(k_store, 'context', split_axis=0, concat_axis=0, tiled=True)]
    unnamed x1 -> x0, blocking collectives: 13.3 us -> none
    gather x4 -> x0, local copies, waits for them, and re-layouts: 7.74 us -> none  [the longest x3 6.55 us: settle(): jnp.take(arrived, inverse, axis=0)]
    dot_general x3 -> x0, matrix products: 6.82 us -> none  [the longest x1 2.51 us: on_device(): jnp.einsum('cthd,chde->cthe', matched, carry_states, preferred_element_ty...]
    all_to_all x1 -> x0, starting transfers between devices: 4.99 us -> none  [on_device(): lax.all_to_all(k_store, 'context', split_axis=0, concat_axis=0, tiled=True)]
  transfers between devices with their start and end apart: 2 -> 0, of which waited for: 2 -> 0; matrix products, arithmetic and copies ran while one was open for 3% -> 0% of each run, Pallas kernels for 0% -> 0%
where the time goes in v1:
time: 106 us
  Pallas kernels  100 us (94%)
  local copies, waits for them, and re-layouts  6.03 us (6%)
    pallas_call x1, Pallas kernels, by_heads(): pl.pallas_call(functools.partial(heads_kernel, n, heads), out_shape=jax.S...  100 us
    unnamed x13, local copies, waits for them, and re-layouts  6.03 us

profile of v1, /device:TPU:0, one launch (start us, length us, event | category | flops | bytes accessed | tf_op | source)
XLA Modules:
  0.0 106.1 jit_solution(1733060360281425480)
XLA Ops:
  0.0 0.0 copy-start.4
  0.0 0.0 copy-start.5
  0.0 0.7 copy-done.4
  0.7 0.0 copy-done.5
  0.7 0.0 copy-start
  0.7 1.2 %copy-done = bf16[128,4096]{1,0:T(8,128)(2,1)S(1)} copy-done((bf16[128,4096]{1,0:T(8,128)(2,1)S(1)}, bf16[128,4096]{1,0:T(8,128)(2,1)}, u32[]{:S(2)}) %copy-start) | copy-done | bytes 1048600
  1.9 0.0 copy-start.1
  1.9 1.2 %copy-done.1 = bf16[128,4096]{1,0:T(8,128)(2,1)S(1)} copy-done((bf16[128,4096]{1,0:T(8,128)(2,1)S(1)}, bf16[128,4096]{1,0:T(8,128)(2,1)}, u32[]{:S(2)}) %copy-start.1) | copy-done | bytes 1048600
  3.1 0.0 copy-start.2
  3.1 1.2 %copy-done.2 = bf16[128,4096]{1,0:T(8,128)(2,1)S(1)} copy-done((bf16[128,4096]{1,0:T(8,128)(2,1)S(1)}, bf16[128,4096]{1,0:T(8,128)(2,1)}, u32[]{:S(2)}) %copy-start.2) | copy-done | bytes 1048600
  4.3 0.0 copy-start.3
  4.3 0.7 copy-done.3
  5.1 100.0 %shard_map.64 = bf16[128,4096]{1,0:T(8,128)(2,1)S(1)} custom-call(bf16[128,4096]{1,0:T(8,128)(2,1)S(1)} %copy-done, bf16[128,4096]{1,0:T(8,128)(2,1)S(1)} %copy-done.1, bf16[128,4096]{1,0:T(8,128)(2,1)S(1)} %copy-done.2, s32[1,128]{1,0:T(1,128)S(1)} %copy-done.4, s32[1,128]{1,0:T(1,128)S(1)} %bitcast.3, f32[32,128]{1,0:T(8,128)S(1)} %bitcast.2), custom_call_target="tpu_custom_call" | custom-call | flops 805306368 | bytes 4194304 | tf_op jit(solution)/shard_map/pallas_call | solution.py:171
  105.1 1.0 copy.8
Async XLA Ops:
  0.0 0.7 copy-start.4
  0.0 0.7 copy-start.5
  0.7 1.2 %copy-start = (bf16[128,4096]{1,0:T(8,128)(2,1)S(1)}, bf16[128,4096]{1,0:T(8,128)(2,1)}, u32[]{:S(2)}) copy-start(bf16[128,4096]{1,0:T(8,128)(2,1)} %q_ref.1) | copy-start | bytes 3145732
  1.9 1.2 %copy-start.1 = (bf16[128,4096]{1,0:T(8,128)(2,1)S(1)}, bf16[128,4096]{1,0:T(8,128)(2,1)}, u32[]{:S(2)}) copy-start(bf16[128,4096]{1,0:T(8,128)(2,1)} %k_ref.1) | copy-start | bytes 3145732
  3.1 1.2 %copy-start.2 = (bf16[128,4096]{1,0:T(8,128)(2,1)S(1)}, bf16[128,4096]{1,0:T(8,128)(2,1)}, u32[]{:S(2)}) copy-start(bf16[128,4096]{1,0:T(8,128)(2,1)} %v_ref.1) | copy-start | bytes 3145732
  4.3 0.7 copy-start.3

commit v2 on v1

--- a/solution.py
+++ b/solution.py
@@ -23,24 +23,77 @@
 
 
 def heads_kernel(
-    n, heads, q_ref, k_ref, v_ref, plan_ref, docs_ref, gain_ref, out_ref,
-    got, leaving, info, mask, tail, match, keep, send_sem, got_sem, info_sem, out_sem,
+    n, heads, q_hbm, k_hbm, v_hbm, plan_hbm, docs_hbm, gain_hbm, out_ref,
+    plan_ref, docs_ref, gain_ref, packed, got, leaving, info, mask, tail, match, keep,
+    load_sem, small_sem, send_sem, got_sem, info_sem, out_sem,
 ):
-    tokens = q_ref.shape[0]
+    tokens = q_hbm.shape[0]
     share = tokens // n
     blocks = TILE // share
     rows = n * TILE
     chunks = tokens // TILE
     me = lax.axis_index("context")
     f32, bf16 = jnp.float32, jnp.bfloat16
+    stride = n // 2 + 1 if n > 2 else 1
+
+    def partner(step):
+        return flip(me, (step * stride) % n, n)
+
+    def columns(device, g):
+        return pl.ds(pl.multiple_of((device * heads + g) * HEAD_DIM, HEAD_DIM), HEAD_DIM)
+
+    def load(g):
+        @pl.loop(1, n)
+        def _(step):
+            to = partner(step)
+            for a, ref in enumerate((q_hbm, k_hbm, v_hbm)):
+                pltpu.make_async_copy(
+                    ref.at[:, columns(to, g)], packed.at[g, to, a], load_sem.at[g, to]
+                ).start()
+
+    def send(g):
+        @pl.loop(1, n)
+        def _(step):
+            to = partner(step)
+            pltpu.make_async_copy(packed.at[g, to], packed.at[g, to], load_sem.at[g, to]).wait()
+            pltpu.make_async_remote_copy(
+                src_ref=packed.at[g, to], dst_ref=got.at[g, me],
+                send_sem=send_sem.at[g], recv_sem=got_sem.at[g],
+                device_id={"context": to}, device_id_type=MESH,
+            ).start()
+
+    def own(g):
+        for a, ref in enumerate((q_hbm, k_hbm, v_hbm)):
+            pltpu.make_async_copy(
+                ref.at[:, columns(me, g)], got.at[g, me, a], got_sem.at[g]
+            ).start()
 
     barrier = pltpu.get_barrier_semaphore()
 
     @pl.loop(1, n)
     def _(step):
         pl.semaphore_signal(
-            barrier, inc=1, device_id={"context": flip(me, step, n)}, device_id_type=MESH
+            barrier, inc=1, device_id={"context": partner(step)}, device_id_type=MESH
         )
+
+    load(0)
+    small = [
+        pltpu.make_async_copy(source, target, small_sem.at[i])
+        for i, (source, target) in enumerate(
+            ((plan_hbm, plan_ref), (docs_hbm, docs_ref), (gain_hbm, gain_ref))
+        )
+    ]
+    for copy in small:
+        copy.start()
+
+    pl.semaphore_wait(barrier, n - 1)
+    send(0)
+    for g in range(1, heads):
+        load(g)
+    for g in range(heads):
+        own(g)
+    for copy in small:
+        copy.wait()
 
     plan = plan_ref[...]
     here = lax.broadcasted_iota(jnp.int32, (tokens, tokens), 0) == plan
@@ -66,36 +119,16 @@
     )
     info[me] = spread_lines + base
 
-    pl.semaphore_wait(barrier, n - 1)
-
     @pl.loop(1, n)
     def _(step):
-        to = flip(me, step, n)
         pltpu.make_async_remote_copy(
             src_ref=info.at[me], dst_ref=info.at[me],
             send_sem=info_sem.at[0], recv_sem=info_sem.at[1],
-            device_id={"context": to}, device_id_type=MESH,
+            device_id={"context": partner(step)}, device_id_type=MESH,
         ).start()
 
-    def columns(device, g):
-        return pl.ds(pl.multiple_of((device * heads + g) * HEAD_DIM, HEAD_DIM), HEAD_DIM)
-
-    for g in range(heads):
-
-        @pl.loop(1, n)
-        def _(step, g=g):
-            to = flip(me, (step * 7) % n, n)
-            for a, ref in enumerate((q_ref, k_ref, v_ref)):
-                pltpu.make_async_remote_copy(
-                    src_ref=ref.at[:, columns(to, g)], dst_ref=got.at[g, a, me],
-                    send_sem=send_sem.at[g], recv_sem=got_sem.at[g],
-                    device_id={"context": to}, device_id_type=MESH,
-                ).start()
-
-        for a, ref in enumerate((q_ref, k_ref, v_ref)):
-            pltpu.make_async_copy(
-                ref.at[:, columns(me, g)], got.at[g, a, me], got_sem.at[g]
-            ).start()
+    for g in range(1, heads):
+        send(g)
 
     def wait_for(ref, sem):
         pltpu.make_async_copy(ref, ref, sem).wait()
@@ -124,9 +157,9 @@
         state = jnp.zeros((HEAD_DIM, HEAD_DIM), f32)
         for c in range(chunks):
             part = pl.ds(c * TILE, TILE)
-            q = got[g, 0, :, part, :].reshape(rows, HEAD_DIM)
-            k = got[g, 1, :, part, :].reshape(rows, HEAD_DIM)
-            v = got[g, 2, :, part, :].reshape(rows, HEAD_DIM)
+            q = got[g, :, 0, part, :].reshape(rows, HEAD_DIM)
+            k = got[g, :, 1, part, :].reshape(rows, HEAD_DIM)
+            v = got[g, :, 2, part, :].reshape(rows, HEAD_DIM)
             scores = lax.dot_general(q, k, (((1,), (1,)), ((), ())), preferred_element_type=f32)
             weights = scores.astype(bf16) * mask[c]
             mixed = jnp.dot(weights, v, preferred_element_type=f32)
@@ -145,7 +178,7 @@
 
         @pl.loop(1, n)
         def _(step, g=g):
-            to = flip(me, (step * 7) % n, n)
+            to = partner(step)
             pltpu.make_async_remote_copy(
                 src_ref=leaving.at[g, to], dst_ref=out_ref.at[:, columns(me, g)],
                 send_sem=send_sem.at[heads + g], recv_sem=out_sem.at[g],
@@ -158,7 +191,7 @@
 
     wait_for(info.at[pl.ds(0, n - 1)], info_sem.at[0])
     for g in range(heads):
-        wait_for(got.at[g, :, pl.ds(0, n - 1)], send_sem.at[g])
+        wait_for(got.at[g, pl.ds(0, n - 1)], send_sem.at[g])
         wait_for(leaving.at[g, pl.ds(0, n - 1)], send_sem.at[heads + g])
         wait_for(leaving.at[g], out_sem.at[g])
 
@@ -171,23 +204,29 @@
     return pl.pallas_call(
         functools.partial(heads_kernel, n, heads),
         out_shape=jax.ShapeDtypeStruct((tokens, width), bf16),
-        in_specs=[pl.BlockSpec(memory_space=pltpu.VMEM)] * 6,
-        out_specs=pl.BlockSpec(memory_space=pltpu.VMEM),
+        in_specs=[pl.BlockSpec(memory_space=pltpu.HBM)] * 6,
+        out_specs=pl.BlockSpec(memory_space=pltpu.HBM),
         scratch_shapes=[
-            pltpu.VMEM((heads, 3, n, tokens, HEAD_DIM), bf16),
+            pltpu.VMEM((1, tokens), jnp.int32),
+            pltpu.VMEM((1, tokens), jnp.int32),
+            pltpu.VMEM((width // HEAD_DIM, HEAD_DIM), f32),
+            pltpu.VMEM((heads, n, 3, tokens, HEAD_DIM), bf16),
+            pltpu.VMEM((heads, n, 3, tokens, HEAD_DIM), bf16),
             pltpu.VMEM((heads, n, tokens, HEAD_DIM), bf16),
             pltpu.VMEM((n, 8, rows), f32),
             pltpu.VMEM((chunks, rows, rows), bf16),
             pltpu.VMEM((chunks, rows, HEAD_DIM), bf16),
             pltpu.VMEM((chunks, rows, HEAD_DIM), bf16),
             pltpu.VMEM((chunks, 8, HEAD_DIM), f32),
+            pltpu.SemaphoreType.DMA((heads, n)),
+            pltpu.SemaphoreType.DMA((3,)),
             pltpu.SemaphoreType.DMA((2 * heads,)),
             pltpu.SemaphoreType.DMA((heads,)),
             pltpu.SemaphoreType.DMA((2,)),
             pltpu.SemaphoreType.DMA((heads,)),
         ],
         compiler_params=pltpu.CompilerParams(
-            collective_id=0, has_side_effects=True, vmem_limit_bytes=40 * 1024 * 1024
+            collective_id=0, has_side_effects=True, vmem_limit_bytes=63 * 1024 * 1024
         ),
         cost_estimate=pl.CostEstimate(
             flops=2 * heads * n * tokens * HEAD_DIM * (2 * rows + 2 * HEAD_DIM),

time: 106 us -> 103 us (0.972)
  local copies, waits for them, and re-layouts: 6.03 us -> 2.29 us
    unnamed x13 -> x1, local copies, waits for them, and re-layouts: 6.03 us -> 2.29 us
where the time goes in v2:
time: 103 us; the launch traced here: 102 us
  Pallas kernels  100 us (97%)
  local copies, waits for them, and re-layouts  2.29 us (2%)
    pallas_call x1, Pallas kernels, by_heads(): pl.pallas_call(functools.partial(heads_kernel, n, heads), out_shape=jax.S...  100 us
    unnamed x1, local copies, waits for them, and re-layouts  2.29 us

profile of v2, /device:TPU:0, one launch (start us, length us, event | category | flops | bytes accessed | tf_op | source)
XLA Modules:
  0.0 102.3 jit_solution(7635920140358337999)
XLA Ops:
  0.0 100.0 %shard_map.64 = bf16[128,4096]{1,0:T(8,128)(2,1)} custom-call(bf16[128,4096]{1,0:T(8,128)(2,1)} %q_hbm.1, bf16[128,4096]{1,0:T(8,128)(2,1)} %k_hbm.1, bf16[128,4096]{1,0:T(8,128)(2,1)} %v_hbm.1, s32[1,128]{1,0:T(1,128)} %plan_hbm.1, s32[1,128]{1,0:T(1,128)} %bitcast.3, f32[32,128]{1,0:T(8,128)} %bitcast.2), custom_call_target="tpu_custom_call" | custom-call | flops 805306368 | bytes 4194304 | tf_op jit(solution)/shard_map/pallas_call | solution.py:204
  100.0 2.3 %copy.8 = bf16[128,4096]{1,0:T(8,128)(2,1)} copy(bf16[128,4096]{1,0:T(8,128)(2,1)} %shard_map.64) | data formatting | bytes 2097152

commit v3 on v2

--- a/solution.py
+++ b/solution.py
@@ -205,7 +205,7 @@
         functools.partial(heads_kernel, n, heads),
         out_shape=jax.ShapeDtypeStruct((tokens, width), bf16),
         in_specs=[pl.BlockSpec(memory_space=pltpu.HBM)] * 6,
-        out_specs=pl.BlockSpec(memory_space=pltpu.HBM),
+        out_specs=pl.BlockSpec(memory_space=pltpu.VMEM),
         scratch_shapes=[
             pltpu.VMEM((1, tokens), jnp.int32),
             pltpu.VMEM((1, tokens), jnp.int32),
@@ -226,7 +226,7 @@
             pltpu.SemaphoreType.DMA((heads,)),
         ],
         compiler_params=pltpu.CompilerParams(
-            collective_id=0, has_side_effects=True, vmem_limit_bytes=63 * 1024 * 1024
+            collective_id=0, has_side_effects=True, vmem_limit_bytes=52 * 1024 * 1024
         ),
         cost_estimate=pl.CostEstimate(
             flops=2 * heads * n * tokens * HEAD_DIM * (2 * rows + 2 * HEAD_DIM),

time: 103 us -> 102 us (level)
    unnamed x1 -> x7, local copies, waits for them, and re-layouts: 2.29 us -> 2.36 us
where the time goes in v3:
time: 102 us
  Pallas kernels  99.4 us (97%)
  local copies, waits for them, and re-layouts  2.36 us (2%)
    pallas_call x1, Pallas kernels, by_heads(): pl.pallas_call(functools.partial(heads_kernel, n, heads), out_shape=jax.S...  99.4 us
    unnamed x7, local copies, waits for them, and re-layouts  2.36 us

profile of v3, /device:TPU:0, one launch (start us, length us, event | category | flops | bytes accessed | tf_op | source)
XLA Modules:
  0.0 101.8 jit_solution(2590738120290396106)
XLA Ops:
  0.0 0.0 copy-start.1
  0.0 0.0 copy-start.2
  0.0 0.7 copy-done.1
  0.7 0.0 copy-done.2
  0.7 0.0 copy-start
  0.7 0.7 copy-done
  1.4 99.4 %shard_map.64 = bf16[128,4096]{1,0:T(8,128)(2,1)S(1)} custom-call(bf16[128,4096]{1,0:T(8,128)(2,1)} %q_hbm.1, bf16[128,4096]{1,0:T(8,128)(2,1)} %k_hbm.1, bf16[128,4096]{1,0:T(8,128)(2,1)} %v_hbm.1, s32[1,128]{1,0:T(1,128)S(1)} %copy-done.1, s32[1,128]{1,0:T(1,128)S(1)} %bitcast.3, f32[32,128]{1,0:T(8,128)S(1)} %bitcast.2), custom_call_target="tpu_custom_call" | custom-call | flops 805306368 | bytes 4194304 | tf_op jit(solution)/shard_map/pallas_call | solution.py:204
  100.8 1.0 copy.8
Async XLA Ops:
  0.0 0.7 copy-start.1
  0.0 0.7 copy-start.2
  0.7 0.7 copy-start
